TPU v7x, 32 devices: a whole 2x2x4 slice. The times are simulated.
32 devices in a mesh: member: 2 (over y), lat: 4 (over z), lon: 2 (over x), sub: 2 (over core).
Axes of the slice: x: 2, y: 2, z: 4, core: 2. Of those that a mesh axis runs over, the one named last changes fastest.
Arguments:
- grid_latent: bfloat16 [64, 128, 512], P(('member', 'lat'), 'lon'), parts along dimension 0, may hold values from -6 to 6
- mesh_latent: bfloat16 [4096, 512], P(('member', 'lat', 'lon')), parts along dimension 0, may hold values from -6 to 6
- g2m_sender: int32 [8192], P(('lat', 'lon')), may hold values from 0 to 1151
- g2m_receiver: int32 [8192], P(('lat', 'lon')), may hold values from 0 to 255
- g2m_feature: float32 [4, 8192], P(None, ('lat', 'lon')), may hold values from -5 to 5
- tile_count: int32 [16], P(('lat', 'lon')), may hold values from 1 to 32, as said below
- mesh_send: int32 [512], P(('lat', 'lon')), may hold values from 0 to 255
- m2m_sender: int32 [32768], P(('lat', 'lon')), may hold values from 0 to 319, as said below
- m2m_receiver: int32 [32768], P(('lat', 'lon')), may hold values from 0 to 255
- m2m_feature: float32 [4, 32768], P(None, ('lat', 'lon')), may hold values from -5 to 5
- sender_w: bfloat16 [2, 512, 512], P(None, None, 'sub'), may hold values from -0.25 to 0.25
- receiver_w: bfloat16 [2, 512, 512], P(None, None, 'sub'), may hold values from -0.25 to 0.25
- edge_w: float32 [2, 4, 512], P(None, None, 'sub'), may hold values from -3 to 3
- edge_bias: float32 [2, 512], P(None, 'sub'), may hold values from -4 to 4
- msg_w: bfloat16 [2, 512, 512], P(None, 'sub'), may hold values from -0.25 to 0.25
- node_w: bfloat16 [2, 1024, 512], P(None, None, 'sub'), may hold values from -0.1875 to 0.1875
- node_bias: float32 [2, 512], P(None, 'sub'), may hold values from -4 to 4
- node_out: bfloat16 [2, 512, 512], P(None, 'sub'), may hold values from -0.25 to 0.25
- node_gain: float32 [2, 512], replicated, may hold values from 0.5 to 1.5
Outputs:
- mesh_out: bfloat16 [4096, 512], P(('member', 'lat', 'lon')), parts along dimension 0
There are 2 independent parts, one for each index of `member`. A program takes and returns all parts, laid end to end along the dimension named above; an argument that names none is the same for every part. Nothing has to cross between parts.
Inputs may be any that keep to these rules, and one draw needn't show every extreme that they name: `tile_count`: entries 2 p and 2 p + 1 count the live g2m and m2m tiles of patch p, the first at most 8, the second at most 32; each bound is reached by some patch. `m2m_sender`: a sender below 256 is a node of the patch itself; a sender 256 + p * 8 + c read by patch q has c < 2, or p is a neighbour of q: its latitude band differs by at most one and its longitude band by at most one modulo 2, and p != q.
All inputs are finite; a program needn't handle non-finite values.
Results may differ from a plain program's by a relative error of at most 0.0075.
Values may be sent and summed in bfloat16 or wider, within the bound.
A program may use at most 64 MiB of HBM per device.

v0:
```python
import math

import jax
import jax.numpy as jnp
from jax import lax
from jax.sharding import PartitionSpec as P

HALO = 4
TILE = 128


def extended(cells, sides, width, closed):
    for axis, dim in sides:
        count = lax.axis_size(axis)
        ends = count if closed else count - 1
        head = lax.slice_in_dim(cells, 0, width, axis=dim)
        tail = lax.slice_in_dim(cells, cells.shape[dim] - width, cells.shape[dim], axis=dim)
        cells = jnp.concatenate(
            [
                lax.ppermute(tail, axis, [(i, (i + 1) % count) for i in range(ends)]),
                cells,
                lax.ppermute(head, axis, [((i + 1) % count, i) for i in range(ends)]),
            ],
            axis=dim,
        )
    return cells


def layer_norm(values):
    average = jnp.mean(values, axis=-1, keepdims=True)
    centred = values - average
    variance = jnp.mean(centred * centred, axis=-1, keepdims=True)
    return centred * lax.rsqrt(variance + 1e-05)


def edge_sums(
    sender_table,
    recv_proj,
    senders,
    receivers,
    features,
    live_tiles,
    edge_weight,
    edge_offset,
    msg_weight,
):
    total_tiles = senders.shape[0] // TILE
    step_tiles = math.gcd(4, total_tiles)
    span = step_tiles * TILE
    node_count = recv_proj.shape[0]
    node_ids = jnp.arange(node_count, dtype=jnp.int32)[:, None]
    live_edges = live_tiles * TILE

    def one_block(block_number, running):
        block_start = block_number * span
        send_ids = lax.dynamic_slice_in_dim(senders, block_start, span)
        recv_ids = lax.dynamic_slice_in_dim(receivers, block_start, span)
        edge_feats = lax.dynamic_slice_in_dim(features, block_start, span, 1)
        preact = sender_table[send_ids].astype(jnp.float32) + recv_proj[recv_ids]
        preact = (
            preact
            + jnp.dot(
                edge_feats.T,
                edge_weight,
                precision=lax.Precision.HIGHEST,
                preferred_element_type=jnp.float32,
            )
            + edge_offset
        )
        hidden = jax.nn.silu(preact).astype(jnp.bfloat16)
        messages = jnp.dot(hidden, msg_weight, preferred_element_type=jnp.float32)
        edge_ids = block_start + jnp.arange(span, dtype=jnp.int32)
        selector = ((recv_ids[None, :] == node_ids) & (edge_ids[None, :] < live_edges)).astype(
            jnp.float32
        )
        return running + jnp.dot(
            selector, messages, precision=lax.Precision.HIGHEST, preferred_element_type=jnp.float32
        )

    initial = jnp.zeros((node_count, msg_weight.shape[1]), jnp.float32)
    block_total = (live_tiles + step_tiles - 1) // step_tiles
    return lax.fori_loop(0, block_total, one_block, initial)


def width_sum(partial_value):
    return lax.psum(partial_value, "sub")


def node_update(latent, inbound, node_weight, node_offset, out_weight, gain_row):
    joined = jnp.concatenate([latent, inbound.astype(jnp.bfloat16)], axis=1)
    hidden = jax.nn.silu(
        jnp.dot(joined, node_weight, preferred_element_type=jnp.float32) + node_offset
    ).astype(jnp.bfloat16)
    node_sum = width_sum(jnp.dot(hidden, out_weight, preferred_element_type=jnp.float32))
    return (latent.astype(jnp.float32) + layer_norm(node_sum) * gain_row).astype(jnp.bfloat16)


def extend(features):
    lon_wide = extended(features, (("lon", 1),), HALO, True)
    return extended(lon_wide, (("lat", 0),), HALO, False)


def route(outgoing):
    return lax.all_to_all(outgoing, ("lat", "lon"), split_axis=0, concat_axis=0, tiled=True)


def body(
    grid_latent,
    mesh_latent,
    g2m_sender,
    g2m_receiver,
    g2m_feature,
    tile_count,
    mesh_send,
    m2m_sender,
    m2m_receiver,
    m2m_feature,
    sender_w,
    receiver_w,
    edge_w,
    edge_bias,
    msg_w,
    node_w,
    node_bias,
    node_out,
    node_gain,
):
    grid_rows, grid_cols, latent_width = grid_latent.shape
    hidden_half = sender_w.shape[2]
    projected = jnp.dot(
        grid_latent.reshape(-1, latent_width), sender_w[0], preferred_element_type=jnp.float32
    )
    projected = projected.astype(jnp.bfloat16).reshape(grid_rows, grid_cols, hidden_half)
    window = extend(projected).reshape(-1, hidden_half)
    receiver_mesh = jnp.dot(mesh_latent, receiver_w[0], preferred_element_type=jnp.float32)
    encoded = edge_sums(
        window,
        receiver_mesh,
        g2m_sender,
        g2m_receiver,
        g2m_feature,
        tile_count[0],
        edge_w[0],
        edge_bias[0],
        msg_w[0],
    )
    inbound = width_sum(encoded)
    mesh_mid = node_update(mesh_latent, inbound, node_w[0], node_bias[0], node_out[0], node_gain[0])
    patch_count = lax.axis_size("lat") * lax.axis_size("lon")
    send_lists = mesh_send.reshape(patch_count, -1)
    sender_mesh = jnp.dot(mesh_mid, sender_w[1], preferred_element_type=jnp.float32).astype(
        jnp.bfloat16
    )
    received = route(sender_mesh[send_lists]).reshape(-1, hidden_half)
    sender_table = jnp.concatenate([sender_mesh, received], axis=0)
    receiver_mid = jnp.dot(mesh_mid, receiver_w[1], preferred_element_type=jnp.float32)
    processed = edge_sums(
        sender_table,
        receiver_mid,
        m2m_sender,
        m2m_receiver,
        m2m_feature,
        tile_count[1],
        edge_w[1],
        edge_bias[1],
        msg_w[1],
    )
    inbound_mid = width_sum(processed)
    return node_update(mesh_mid, inbound_mid, node_w[1], node_bias[1], node_out[1], node_gain[1])


def solution(mesh):
    placed = (
        P(("member", "lat"), "lon", None),
        P(("member", "lat", "lon"), None),
        P(("lat", "lon")),
        P(("lat", "lon")),
        P(None, ("lat", "lon")),
        P(("lat", "lon")),
        P(("lat", "lon")),
        P(("lat", "lon")),
        P(("lat", "lon")),
        P(None, ("lat", "lon")),
        P(None, None, "sub"),
        P(None, None, "sub"),
        P(None, None, "sub"),
        P(None, "sub"),
        P(None, "sub", None),
        P(None, None, "sub"),
        P(None, "sub"),
        P(None, "sub", None),
        P(),
    )
    return jax.shard_map(
        body,
        mesh=mesh,
        in_specs=placed,
        out_specs=P(("member", "lat", "lon"), None),
        check_vma=False,
    )
```

profile of v0, /device:TPU:0, one launch (start us, length us, event | category | flops | bytes accessed | tf_op | source)
XLA Modules:
  0.0 170.4 jit_solution(16374989147356252350)
XLA Ops:
  7.6 1.3 convolution_convert_fusion
  9.0 3.0 %collective-permute-start = (bf16[8,4,256]{2,1,0:T(4,128)(2,1)S(1)}, bf16[8,4,256]{2,1,0:T(4,128)(2,1)S(1)}, u32[]{:S(2)}, u32[]{:S(2)}) collective-permute-start(bf16[8,4,256]{2,1,0:T(4,128)(2,1)S(1)} %get-tuple-element.255), channel_id=1, source_target_pairs={{0,2},{2,0},{1,3},{3,1},{4,6},{6,4},{5,7},{7,5},{8,10},{10,8},{9,1... | collective-permute-start | bytes 49160 | tf_op jit(solution)/shard_map/ppermute | solution.py:20
  15.9 3.9 %collective-permute-start.2 = (bf16[4,72,256]{2,1,0:T(8,128)(2,1)S(1)}, bf16[4,72,256]{2,1,0:T(8,128)(2,1)S(1)}, u32[]{:S(2)}, u32[]{:S(2)}) collective-permute-start(bf16[4,72,256]{2,1,0:T(8,128)(2,1)S(1)} %get-tuple-element.253), channel_id=1, source_target_pairs={{0,4},{4,8},{8,12},{1,5},{5,9},{9,13},{2,6},{6,10},{10,14},{3,7},{... | collective-permute-start | bytes 442376 | tf_op jit(solution)/shard_map/ppermute | solution.py:20
  19.8 1.3 collective-permute-start.3
  21.1 1.3 collective-permute-done.2
  22.5 4.4 %collective-permute-done.3 = bf16[4,72,256]{2,1,0:T(8,128)(2,1)S(1)} collective-permute-done((bf16[4,72,256]{2,1,0:T(8,128)(2,1)S(1)}, bf16[4,72,256]{2,1,0:T(8,128)(2,1)S(1)}, u32[]{:S(2)}, u32[]{:S(2)}) %collective-permute-start.3) | collective-permute-done | bytes 147488 | tf_op jit(solution)/shard_map/ppermute | solution.py:22
  27.0 11.0 %while.22 = (s32[]{:T(128)}, f32[256,512]{1,0:T(8,128)S(1)}, s32[]{:T(128)}, s32[1024]{0:T(1024)S(1)}, s32[]{:T(128)}, /*index=5*/s32[1024]{0:T(1024)S(1)}, bf16...) while((s32[]{:T(128)}, f32[256,512]{1,0:T(8,128)S(1)}, ...), condition=%wide.region_1.2_spmd.clone, body=%wide.region_0.1_spmd.clone.sunk | while | flops 947394560 | bytes 6334675 | solution.py:82
  27.1 1.6 gather_fusion
  28.7 2.0 %gather_fusion.1 = bf16[512,256]{1,0:T(8,128)(2,1)S(1)} fusion(bf16[1152,256]{1,0:T(8,128)(2,1)S(1)} %get-tuple-element.465, s32[1024]{0:T(1024)S(1)} %pad_clamp_fusion.10), kind=kCustom, calls=%fused_computation.clone.clone.1 | custom fusion | bytes 526336 | tf_op jit(solution)/shard_map/while/body/gather | solution.py:59
  32.6 1.6 gather_fusion
  34.2 2.0 %gather_fusion.1 = bf16[512,256]{1,0:T(8,128)(2,1)S(1)} fusion(bf16[1152,256]{1,0:T(8,128)(2,1)S(1)} %get-tuple-element.465, s32[1024]{0:T(1024)S(1)} %pad_clamp_fusion.10), kind=kCustom, calls=%fused_computation.clone.clone.1 | custom fusion | bytes 526336 | tf_op jit(solution)/shard_map/while/body/gather | solution.py:59
  38.0 4.8 %all-reduce.8 = bf16[256,512]{1,0:T(8,128)(2,1)S(1)} all-reduce(f32[256,512]{1,0:T(8,128)S(1)} %get-tuple-element.141), channel_id=1, replica_groups=mesh['member'=2,'lat'=4,'lon'=2,'sub'=2] {'sub'}, use_global_device_ids=true, to_apply=%region_2.3 | all-reduce | flops 131072 | bytes 786432 | tf_op jit(solution)/shard_map/psum | solution.py:86
  42.9 2.5 %fusion.33 = f32[256,512]{1,0:T(8,128)} fusion(bf16[2,256,512]{2,1,0:T(8,128)(2,1)} %param.40, bf16[2,1024,256]{2,1,0:T(8,128)(2,1)} %param.38, bf16[256,512]{1,0:T(8,128)(2,1)S(1)} %all-reduce.8, bf16[256,512]{1,0:T(8,128)(2,1)S(1)} %copy-done.3, f32[256]{0:T(256)S(1)} %bitcast.100), kind=kOutput, calls=%fused_computation.62 | convolution fusion | flops 202768384 | bytes 1836032 | tf_op jit(solution)/shard_map/dot_general | solution.py:94
  45.5 19.0 %all-reduce.5.cloned.1.call-done = f32[256,512]{1,0:T(8,128)} async-done(((f32[256,512]{1,0:T(8,128)}), f32[256,512]{1,0:T(8,128)}) %all-reduce.5.cloned.1.call-update) | async-done | bytes 524304 | tf_op jit(solution)/shard_map/psum | solution.py:86
  67.5 1.3 gather_fusion.4
  68.8 5.8 %all-to-all-start = ((bf16[8,8,256]{2,1,0:T(8,128)(2,1)}), bf16[8,8,256]{2,1,0:T(8,128)(2,1)S(1)}, u32[]{:S(2)}, u32[]{:S(2)}) async-start(bf16[8,8,256]{2,1,0:T(8,128)(2,1)} %bitcast.16), calls=%async_computation | async-start | bytes 65536 | tf_op jit(solution)/shard_map/all_to_all | solution.py:104
  74.9 6.4 %all-to-all-done = bf16[8,8,256]{2,1,0:T(8,128)(2,1)S(1)} async-done(((bf16[8,8,256]{2,1,0:T(8,128)(2,1)}), bf16[8,8,256]{2,1,0:T(8,128)(2,1)S(1)}, u32[]{:S(2)}, u32[]{:S(2)}) %all-to-all-start) | async-done | bytes 32800 | tf_op jit(solution)/shard_map/all_to_all | solution.py:104
  81.3 7.0 %while.23 = (s32[]{:T(128)}, f32[256,512]{1,0:T(8,128)S(1)}, s32[]{:T(128)}, s32[4096]{0:T(1024)}, s32[]{:T(128)}, /*index=5*/s32[4096]{0:T(1024)}, bf16[320,256...) while((s32[]{:T(128)}, f32[256,512]{1,0:T(8,128)S(1)}, ...), condition=%wide.region_7.8_spmd.clone, body=%wide.region_6.7_spmd.clone.sunk | while | flops 947394560 | bytes 6334675 | solution.py:82
  82.2 1.6 gather_fusion.2
  83.8 2.0 %gather_fusion.3 = bf16[512,256]{1,0:T(8,128)(2,1)S(1)} fusion(bf16[320,256]{1,0:T(8,128)(2,1)S(1)} %get-tuple-element.513, s32[1024]{0:T(1024)S(1)} %pad_clamp_fusion.12), kind=kCustom, calls=%fused_computation.2.clone.clone.1 | custom fusion | bytes 526336 | tf_op jit(solution)/shard_map/while/body/gather | solution.py:59
  85.8 1.4 multiply_convert_fusion.7
  88.3 4.8 %all-reduce.9 = bf16[256,512]{1,0:T(8,128)(2,1)S(1)} all-reduce(f32[256,512]{1,0:T(8,128)S(1)} %get-tuple-element.142), channel_id=1, replica_groups=mesh['member'=2,'lat'=4,'lon'=2,'sub'=2] {'sub'}, use_global_device_ids=true, to_apply=%region_8.9 | all-reduce | flops 131072 | bytes 786432 | tf_op jit(solution)/shard_map/psum | solution.py:86
  93.2 2.4 %fusion.28 = f32[256,512]{1,0:T(8,128)} fusion(bf16[2,256,512]{2,1,0:T(8,128)(2,1)S(1)} %copy-done.16, bf16[2,1024,256]{2,1,0:T(8,128)(2,1)} %param.38, bf16[256,512]{1,0:T(8,128)(2,1)S(1)} %all-reduce.9, bf16[256,512]{1,0:T(8,128)(2,1)S(1)} %add_convert_fusion.1, f32[256]{0:T(256)S(1)} %bitcast.98), kind=kOutput, calls=%fused_computation.57 | convolution fusion | flops 202768384 | bytes 1836032 | tf_op jit(solution)/shard_map/dot_general | solution.py:94
  95.6 64.5 %all-reduce.7.cloned.1.call-done = f32[256,512]{1,0:T(8,128)} async-done(((f32[256,512]{1,0:T(8,128)}), f32[256,512]{1,0:T(8,128)}) %all-reduce.7.cloned.1.call-update) | async-done | bytes 524304 | tf_op jit(solution)/shard_map/psum | solution.py:86
  (93 shorter events, 14.9 us)
Async XLA Ops:
  6.5 5.5 %copy-start.6 = (bf16[2,256,512]{2,1,0:T(8,128)(2,1)S(1)}, bf16[2,256,512]{2,1,0:T(8,128)(2,1)}, u32[]{:S(2)}) copy-start(bf16[2,256,512]{2,1,0:T(8,128)(2,1)} %param.37) | copy-start | bytes 1572868
  6.5 58.0 %all-reduce.5.cloned.1.call-start = ((), (), s32[]{:S(2)}) async-start(), calls=%async_computation.1 | async-start | bytes 1048576 | tf_op jit(solution)/shard_map/psum | solution.py:86
  7.6 4.5 %copy-start.10 = (f32[2,4,256]{2,1,0:T(4,128)S(1)}, f32[2,4,256]{2,1,0:T(4,128)}, u32[]{:S(2)}) copy-start(f32[2,4,256]{2,1,0:T(4,128)} %param.35) | copy-start | bytes 24580
  7.6 4.5 %copy-start.12 = (f32[2,256]{1,0:T(2,128)S(1)}, f32[2,256]{1,0:T(2,128)}, u32[]{:S(2)}) copy-start(f32[2,256]{1,0:T(2,128)} %param.36) | copy-start | bytes 6148
  7.6 4.6 %copy-start.3 = (bf16[256,512]{1,0:T(8,128)(2,1)S(1)}, bf16[256,512]{1,0:T(8,128)(2,1)}, u32[]{:S(2)}) copy-start(bf16[256,512]{1,0:T(8,128)(2,1)} %param.24) | copy-start | bytes 786436
  7.6 4.6 %copy-start.4 = (bf16[2,512,256]{2,1,0:T(8,128)(2,1)S(1)}, bf16[2,512,256]{2,1,0:T(8,128)(2,1)}, u32[]{:S(2)}) copy-start(bf16[2,512,256]{2,1,0:T(8,128)(2,1)} %param.34) | copy-start | bytes 1572868
  8.9 3.5 %copy-start.14 = (s32[2]{0:T(128)S(1)}, s32[2]{0:T(128)}, u32[]{:S(2)}) copy-start(s32[2]{0:T(128)} %param.28) | copy-start | bytes 28
  8.9 6.7 %copy-start.15 = (s32[64]{0:T(128)S(1)}, s32[64]{0:T(128)}, u32[]{:S(2)}) copy-start(s32[64]{0:T(128)} %param.29) | copy-start | bytes 772
  9.0 6.7 %collective-permute-start = (bf16[8,4,256]{2,1,0:T(4,128)(2,1)S(1)}, bf16[8,4,256]{2,1,0:T(4,128)(2,1)S(1)}, u32[]{:S(2)}, u32[]{:S(2)}) collective-permute-start(bf16[8,4,256]{2,1,0:T(4,128)(2,1)S(1)} %get-tuple-element.255), channel_id=1, source_target_pairs={{0,2},{2,0},{1,3},{3,1},{4,6},{6,4},{5,7},{7,5},{8,10},{10,8},{9,1... | collective-permute-start | bytes 49160 | tf_op jit(solution)/shard_map/ppermute | solution.py:20
  12.0 3.7 %collective-permute-start.1 = (bf16[8,4,256]{2,1,0:T(4,128)(2,1)S(1)}, bf16[8,4,256]{2,1,0:T(4,128)(2,1)S(1)}, u32[]{:S(2)}, u32[]{:S(2)}) collective-permute-start(bf16[8,4,256]{2,1,0:T(4,128)(2,1)S(1)} %get-tuple-element.256), channel_id=1, source_target_pairs={{2,0},{0,2},{3,1},{1,3},{6,4},{4,6},{7,5},{5,7},{10,8},{8,10},{11,... | collective-permute-start | bytes 49160 | tf_op jit(solution)/shard_map/ppermute | solution.py:22
  12.1 9.0 %copy-start.13 = (f32[2,256]{1,0:T(2,128)S(1)}, f32[2,256]{1,0:T(2,128)}, u32[]{:S(2)}) copy-start(f32[2,256]{1,0:T(2,128)} %param.39) | copy-start | bytes 6148
  15.8 11.2 %copy-start.8 = (s32[1024]{0:T(1024)S(1)}, s32[1024]{0:T(1024)}, u32[]{:S(2)}) copy-start(s32[1024]{0:T(1024)} %param.26) | copy-start | bytes 12292
  15.8 11.2 %copy-start.9 = (s32[1024]{0:T(1024)S(1)}, s32[1024]{0:T(1024)}, u32[]{:S(2)}) copy-start(s32[1024]{0:T(1024)} %param.25) | copy-start | bytes 12292
  15.8 11.2 %copy-start.17 = (f32[4,1024]{1,0:T(4,128)S(1)}, f32[4,1024]{1,0:T(4,128)}, u32[]{:S(2)}) copy-start(f32[4,1024]{1,0:T(4,128)} %param.27) | copy-start | bytes 49156
  15.9 6.6 %collective-permute-start.2 = (bf16[4,72,256]{2,1,0:T(8,128)(2,1)S(1)}, bf16[4,72,256]{2,1,0:T(8,128)(2,1)S(1)}, u32[]{:S(2)}, u32[]{:S(2)}) collective-permute-start(bf16[4,72,256]{2,1,0:T(8,128)(2,1)S(1)} %get-tuple-element.253), channel_id=1, source_target_pairs={{0,4},{4,8},{8,12},{1,5},{5,9},{9,13},{2,6},{6,10},{10,14},{3,7},{... | collective-permute-start | bytes 442376 | tf_op jit(solution)/shard_map/ppermute | solution.py:20
  19.8 7.0 %collective-permute-start.3 = (bf16[4,72,256]{2,1,0:T(8,128)(2,1)S(1)}, bf16[4,72,256]{2,1,0:T(8,128)(2,1)S(1)}, u32[]{:S(2)}, u32[]{:S(2)}) collective-permute-start(bf16[4,72,256]{2,1,0:T(8,128)(2,1)S(1)} %get-tuple-element.254), channel_id=1, source_target_pairs={{4,0},{8,4},{12,8},{5,1},{9,5},{13,9},{6,2},{10,6},{14,10},{7,3},{... | collective-permute-start | bytes 442376 | tf_op jit(solution)/shard_map/ppermute | solution.py:22
  42.9 2.6 %copy-start.11 = (f32[2,512]{1,0:T(2,128)S(1)}, f32[2,512]{1,0:T(2,128)}, u32[]{:S(2)}) copy-start(f32[2,512]{1,0:T(2,128)} %param.41) | copy-start | bytes 12292
  45.5 21.7 %copy-start.7 = (bf16[2,512,256]{2,1,0:T(8,128)(2,1)S(1)}, bf16[2,512,256]{2,1,0:T(8,128)(2,1)}, u32[]{:S(2)}) copy-start(bf16[2,512,256]{2,1,0:T(8,128)(2,1)} %param.33) | copy-start | bytes 1572868
  64.5 2.5 %copy-start.1 = (f32[256,512]{1,0:T(8,128)S(1)}, f32[256,512]{1,0:T(8,128)}, u32[]{:S(2)}) copy-start(f32[256,512]{1,0:T(8,128)} %all-reduce.5.cloned.1.call-done) | copy-start | bytes 1572868
  67.0 7.6 %copy-start.5 = (bf16[2,512,256]{2,1,0:T(8,128)(2,1)S(1)}, bf16[2,512,256]{2,1,0:T(8,128)(2,1)}, u32[]{:S(2)}) copy-start(bf16[2,512,256]{2,1,0:T(8,128)(2,1)} %param.34) | copy-start | bytes 1572868
  68.8 12.5 %all-to-all-start = ((bf16[8,8,256]{2,1,0:T(8,128)(2,1)}), bf16[8,8,256]{2,1,0:T(8,128)(2,1)S(1)}, u32[]{:S(2)}, u32[]{:S(2)}) async-start(bf16[8,8,256]{2,1,0:T(8,128)(2,1)} %bitcast.16), calls=%async_computation | async-start | bytes 65536 | tf_op jit(solution)/shard_map/all_to_all | solution.py:104
  74.6 85.6 %all-reduce.7.cloned.1.call-start = ((), (), s32[]{:S(2)}) async-start(), calls=%async_computation.2 | async-start | bytes 1048576 | tf_op jit(solution)/shard_map/psum | solution.py:86
  81.3 11.8 %copy-start.16 = (bf16[2,256,512]{2,1,0:T(8,128)(2,1)S(1)}, bf16[2,256,512]{2,1,0:T(8,128)(2,1)}, u32[]{:S(2)}) copy-start(bf16[2,256,512]{2,1,0:T(8,128)(2,1)} %param.40) | copy-start | bytes 1572868
  160.1 2.5 %copy-start.2 = (f32[256,512]{1,0:T(8,128)S(1)}, f32[256,512]{1,0:T(8,128)}, u32[]{:S(2)}) copy-start(f32[256,512]{1,0:T(8,128)} %all-reduce.7.cloned.1.call-done) | copy-start | bytes 1572868
  (1 other events, 1.0 us)
Sparse Core Ops, SparseCore 0:
  45.5 18.9 all-reduce.4
  95.7 64.3 all-reduce.6
where the time goes:
time: 172 us; the launch traced here: 170 us
  waiting for transfers between devices  95.7 us (56%)
  between operations  16.3 us (9%)
  starting transfers between devices  14.1 us (8%)
  local copies, waits for them, and re-layouts  14 us (8%)
  matrix products  13 us (8%)
  blocking collectives  9.65 us (6%)
  other arithmetic  7.26 us (4%)
    psum x2, waiting for transfers between devices, width_sum(): return lax.psum(partial_value, 'sub')  83.6 us
    gather x6, local copies, waits for them, and re-layouts, one_block(): preact = sender_table[send_ids].astype(jnp.float32) + recv_proj[recv_ids]  10.6 us
    psum x2, blocking collectives, width_sum(): return lax.psum(partial_value, 'sub')  9.65 us
    ppermute x2, starting transfers between devices, extended(): lax.ppermute(tail, axis, [(i, (i + 1) % count) for i in range(ends)])  6.93 us
    all_to_all x1, waiting for transfers between devices, route(): lax.all_to_all(outgoing, ('lat', 'lon'), split_axis=0, concat_axis=0, til...  6.39 us
    all_to_all x1, starting transfers between devices, route(): lax.all_to_all(outgoing, ('lat', 'lon'), split_axis=0, concat_axis=0, til...  5.78 us
    dot_general x2, matrix products, node_update(): jnp.dot(hidden, out_weight, preferred_element_type=jnp.float32)  4.89 us
    ppermute x2, waiting for transfers between devices, extended(): lax.ppermute(head, axis, [((i + 1) % count, i) for i in range(ends)])  4.41 us
  transfers between devices with their start and end apart: 7, of which 5 were waited for; matrix products, arithmetic and copies ran while one was open for 1% of the time, Pallas kernels for 0%

commit v1 on v0

v1 whole, which is shorter than its diff:
```python
import functools

import jax
import jax.numpy as jnp
from jax import lax
from jax.experimental import pallas as pl
from jax.experimental.pallas import tpu as pltpu
from jax.sharding import PartitionSpec as P

HALO = 4
TILE = 128
FEAT_ROWS = 16
MESH = pl.DeviceIdType.MESH
BF = jnp.bfloat16
F32 = jnp.float32


def dot(a, b):
    return lax.dot_general(a, b, (((1,), (0,)), ((), ())), preferred_element_type=F32)


def dot_tn(a, b):
    return lax.dot_general(a, b, (((0,), (0,)), ((), ())), preferred_element_type=F32)


def dot_nt(a, b):
    return lax.dot_general(a, b, (((1,), (1,)), ((), ())), preferred_element_type=F32)


def silu(v):
    h = 0.5 * v
    return h + h * jnp.tanh(h)


def one_hot(ids, rows, first=0):
    numbers = lax.broadcasted_iota(jnp.int32, (rows, ids.shape[1]), 0) + first
    return jnp.where(numbers == ids, 1.0, 0.0).astype(BF)


def split(v):
    high = v.astype(BF).astype(F32)
    return high, v - high


def layer_norm(values):
    average = jnp.mean(values, axis=-1, keepdims=True)
    centred = values - average
    variance = jnp.mean(centred * centred, axis=-1, keepdims=True)
    return centred * lax.rsqrt(variance + 1e-05)


def kernel(
    dims,
    grid_h, mesh_h, snd1_h, rcv1_h, feat1_h, tiles_h, lists_h, snd2_h, rcv2_h, feat2_h,
    sw_h, rw_h, ew_h, eb_h, mw_h, nw_h, nb_h, no_h, gain_h,
    out_ref,
    grid, mesh, snd1, rcv1, feat1, tiles, lists, snd2, rcv2, feat2,
    sw, rw, ew, eb, mw, nw, nb, no, gain,
    table1, halo, pack, hot1, hot1h, pre1, fs1,
    table2, listed, arrived, hot2, hot2l, pre2, fs2, wf,
    sums, local_sem, weight_send, weight_recv, halo_send, halo_recv, sum_send, sum_recv,
    list_send, list_recv,
):
    bands, lons, gy, gx, cap = dims
    patches = bands * lons
    lat, lon, sub = lax.axis_index("lat"), lax.axis_index("lon"), lax.axis_index("sub")
    me = lat * lons + lon
    peer = {"sub": 1 - sub}
    cells = gy * gx
    nodes = mesh.shape[0]
    edges1, edges2 = snd1.shape[1], snd2.shape[1]

    pairs = [
        (grid_h, grid), (sw_h.at[0], sw.at[0]), (mesh_h, mesh), (rw_h.at[0], rw.at[0]),
        (snd1_h, snd1), (rcv1_h, rcv1), (feat1_h, feat1), (tiles_h, tiles), (ew_h, ew), (eb_h, eb),
        (snd2_h, snd2), (rcv2_h, rcv2), (feat2_h, feat2), (lists_h, lists),
        (mw_h.at[0], mw.at[0, sub]), (nw_h.at[0], nw.at[0, sub]), (nb_h, nb.at[sub]),
        (no_h.at[0], no.at[0, sub]), (gain_h, gain),
        (sw_h.at[1], sw.at[1]), (rw_h.at[1], rw.at[1]),
        (mw_h.at[1], mw.at[1, sub]), (nw_h.at[1], nw.at[1, sub]), (no_h.at[1], no.at[1, sub]),
    ]
    local = [pltpu.make_async_copy(s, d, local_sem.at[i]) for i, (s, d) in enumerate(pairs)]
    for copy in local:
        copy.start()

    barrier = pltpu.get_barrier_semaphore()
    pl.semaphore_signal(barrier, inc=1, device_id=peer, device_id_type=MESH)
    for k in range(1, patches):
        q = lax.rem(me + k, patches)
        pl.semaphore_signal(
            barrier, inc=1, device_id={"lat": q // lons, "lon": lax.rem(q, lons)}, device_id_type=MESH
        )

    for i in (0, 1):
        local[i].wait()
    table1[0:cells, :] = dot(grid[...], sw[0]).astype(BF)
    side = gy * HALO
    row = lax.broadcasted_iota(jnp.int32, (2 * side, cells), 0)
    col = lax.broadcasted_iota(jnp.int32, (2 * side, cells), 1)
    within = lax.rem(row, side)
    wanted = (within // HALO) * gx + lax.rem(within, HALO) + jnp.where(row >= side, gx - HALO, 0)
    choose = jnp.where(col == wanted, 1.0, 0.0).astype(BF)
    pack[...] = dot(choose, table1[0:cells, :]).astype(BF)

    pl.semaphore_wait(barrier, patches)

    strip = HALO * gx
    half = HALO * HALO
    west = lax.rem(lon + lons - 1, lons)
    east = lax.rem(lon + 1, lons)
    base = 2 * strip
    has_n, has_s = lat > 0, lat < bands - 1

    def halo_copy(i, src, dst, where):
        return pltpu.make_async_remote_copy(
            src_ref=src, dst_ref=halo.at[pl.ds(dst[0], dst[1])], send_sem=halo_send.at[i],
            recv_sem=halo_recv.at[i], device_id=where, device_id_type=MESH,
        )

    north = [
        halo_copy(0, table1.at[pl.ds(0, strip)], (strip, strip), {"lat": lat - 1}),
        halo_copy(1, pack.at[pl.ds(0, half)], (base + 2 * side + 3 * half, half), {"lat": lat - 1, "lon": west}),
        halo_copy(2, pack.at[pl.ds(side, half)], (base + 2 * side + 2 * half, half), {"lat": lat - 1, "lon": east}),
    ]
    south = [
        halo_copy(3, table1.at[pl.ds(cells - strip, strip)], (0, strip), {"lat": lat + 1}),
        halo_copy(4, pack.at[pl.ds(side - half, half)], (base + 2 * side + half, half), {"lat": lat + 1, "lon": west}),
        halo_copy(5, pack.at[pl.ds(2 * side - half, half)], (base + 2 * side, half), {"lat": lat + 1, "lon": east}),
    ]
    across = [
        halo_copy(6, pack.at[pl.ds(0, side)], (base + side, side), {"lon": west}),
        halo_copy(7, pack.at[pl.ds(side, side)], (base, side), {"lon": east}),
    ]

    @pl.when(has_n)
    def _():
        for copy in north:
            copy.start()

    @pl.when(has_s)
    def _():
        for copy in south:
            copy.start()

    for copy in across:
        copy.start()

    weights = [
        pltpu.make_async_remote_copy(
            src_ref=s, dst_ref=d, send_sem=weight_send.at[i], recv_sem=weight_recv.at[i],
            device_id=peer, device_id_type=MESH,
        )
        for i, (s, d) in enumerate(
            [
                (mw_h.at[0], mw.at[0, sub]), (nw_h.at[0], nw.at[0, sub]), (nb_h, nb.at[sub]),
                (no_h.at[0], no.at[0, sub]),
                (mw_h.at[1], mw.at[1, sub]), (nw_h.at[1], nw.at[1, sub]), (no_h.at[1], no.at[1, sub]),
            ]
        )
    ]
    for copy in weights:
        copy.start()

    @pl.when(jnp.logical_not(has_n))
    def _():
        halo[0:strip, :] = jnp.zeros((strip, halo.shape[1]), BF)
        halo[base + 2 * side:base + 2 * side + 2 * half, :] = jnp.zeros((2 * half, halo.shape[1]), BF)

    @pl.when(jnp.logical_not(has_s))
    def _():
        halo[strip:base, :] = jnp.zeros((strip, halo.shape[1]), BF)
        halo[base + 2 * side + 2 * half:base + 2 * side + 4 * half, :] = jnp.zeros(
            (2 * half, halo.shape[1]), BF
        )

    for i in range(2, 14):
        local[i].wait()
    table1[cells:cells + nodes, :] = dot(mesh[...], rw[0]).astype(BF)

    def weight_rows(layer):
        high, low = split(ew[layer])
        wf[0:4, :] = high
        wf[4:8, :] = high
        wf[8:12, :] = low
        high, low = split(eb[pl.ds(layer, 1), :])
        wf[12:13, :] = high
        wf[13:14, :] = low
        wf[14:16, :] = jnp.zeros((2, wf.shape[1]), F32)
        return wf[...].astype(BF)

    def feature_rows(fs, feat):
        high, low = split(feat[...])
        fs[0:4, :] = high
        fs[4:8, :] = low
        fs[8:12, :] = high
        fs[12:16, :] = jnp.ones((4, fs.shape[1]), F32)
        return fs[...].astype(BF)

    table1[cells + nodes:cells + nodes + FEAT_ROWS, :] = weight_rows(0)
    hot1[cells + nodes:cells + nodes + FEAT_ROWS, :] = feature_rows(fs1, feat1)

    def live(ids, which):
        slot = lax.broadcasted_iota(jnp.int32, ids.shape, 1)
        return jnp.where(slot < tiles[0:1, which:which + 1] * TILE, ids, -1)

    wide = gx + 2 * HALO
    place = snd1[...]
    r = place // wide
    c = place - r * wide
    rr, cc = r - HALO, c - HALO
    inside = (cc >= 0) & (cc < gx)
    edge_col = jnp.where(cc < 0, c, cc - gx)
    far_side = jnp.where(cc < 0, 0, 1)
    middle = jnp.where(inside, rr * gx + cc, cells + base + far_side * side + rr * HALO + edge_col)
    upper = jnp.where(inside, cells + r * gx + cc, cells + base + 2 * side + far_side * half + r * HALO + edge_col)
    down = rr - gy
    lower = jnp.where(
        inside,
        cells + strip + down * gx + cc,
        cells + base + 2 * side + (2 + far_side) * half + down * HALO + edge_col,
    )
    place = jnp.where(rr < 0, upper, jnp.where(rr >= gy, lower, middle))
    hot1[0:cells, :] = one_hot(place, cells)
    hot1h[...] = one_hot(place, hot1h.shape[0], cells)
    hot1[cells:cells + nodes, :] = one_hot(live(rcv1[...], 0), nodes)
    pre1[...] = dot_tn(table1[...], hot1[...])

    hot2[2 * nodes:2 * nodes + FEAT_ROWS, :] = feature_rows(fs2, feat2)
    rcv2[...] = live(rcv2[...], 1)
    span = min(512, edges2)

    def select(step, carry):
        at = pl.ds(pl.multiple_of(step * span, span), span)
        ids = snd2[:, at]
        hot2[0:nodes, at] = one_hot(ids, nodes)
        hot2[nodes:2 * nodes, at] = one_hot(rcv2[:, at], nodes)
        source = (ids - nodes) // cap
        turn = me - source
        turn = jnp.where(turn < 0, turn + patches, turn)
        ids = jnp.where(ids < nodes, -1, turn * cap + (ids - nodes) - source * cap)
        hot2l[:, at] = one_hot(ids, patches * cap)
        return carry

    lax.fori_loop(0, edges2 // span, select, 0)

    @pl.when(has_n)
    def _():
        for i in (3, 4, 5):
            south[i - 3].wait_recv()
        for copy in north:
            copy.wait_send()

    @pl.when(has_s)
    def _():
        for copy in north:
            copy.wait_recv()
        for copy in south:
            copy.wait_send()

    for copy in across:
        copy.wait()
    hidden = silu(pre1[...] + dot_tn(halo[...], hot1h[...])).astype(BF)

    def exchange(layer, total):
        sums[layer, sub] = total.astype(BF)
        copy = pltpu.make_async_remote_copy(
            src_ref=sums.at[layer, sub], dst_ref=sums.at[layer, sub], send_sem=sum_send.at[layer],
            recv_sem=sum_recv.at[layer], device_id=peer, device_id_type=MESH,
        )
        copy.start()
        return copy

    def node_update(latent, layer):
        inbound = dot(sums[layer, 0], mw[layer, 0]) + dot(sums[layer, 1], mw[layer, 1])
        joined = jnp.concatenate([latent, inbound.astype(BF)], axis=1)
        total = 0.0
        for j in (0, 1):
            units = silu(dot(joined, nw[layer, j]) + nb[j, layer:layer + 1, :]).astype(BF)
            total = total + dot(units, no[layer, j])
        return (latent.astype(F32) + layer_norm(total) * gain[layer:layer + 1, :]).astype(BF)

    copy = exchange(0, dot_nt(hot1[cells:cells + nodes, :], hidden))
    table2[2 * nodes:2 * nodes + FEAT_ROWS, :] = weight_rows(1)
    for i in range(14, len(local)):
        local[i].wait()
    for other in weights[:4]:
        other.wait()
    copy.wait()
    mid = node_update(mesh[...], 0)

    sender = dot(mid, sw[1]).astype(BF)
    table2[0:nodes, :] = sender
    listed[...] = dot_tn(one_hot(lists[...], nodes), sender).reshape(listed.shape)
    routes = []
    for k in range(1, patches):
        q = lax.rem(me + k, patches)
        routes.append(
            pltpu.make_async_remote_copy(
                src_ref=listed.at[q], dst_ref=arrived.at[k], send_sem=list_send.at[k],
                recv_sem=list_recv.at[k], device_id={"lat": q // lons, "lon": lax.rem(q, lons)},
                device_id_type=MESH,
            )
        )
        routes[-1].start()
    arrived[0] = listed[me]
    table2[nodes:2 * nodes, :] = dot(mid, rw[1]).astype(BF)

    def before(step, carry):
        at = pl.ds(pl.multiple_of(step * span, span), span)
        pre2[:, at] = dot_tn(table2[...], hot2[:, at])
        return carry

    lax.fori_loop(0, edges2 // span, before, 0)
    for route in routes:
        route.wait()
    far = arrived[...].reshape(patches * cap, arrived.shape[2]).astype(BF)

    def after(step, total):
        at = pl.ds(pl.multiple_of(step * span, span), span)
        hidden = silu(pre2[:, at] + dot_tn(far, hot2l[:, at])).astype(BF)
        return total + dot_nt(hot2[nodes:2 * nodes, at], hidden)

    total = lax.fori_loop(0, edges2 // span, after, jnp.zeros((nodes, far.shape[1]), F32))
    copy = exchange(1, total)
    for other in weights[4:]:
        other.wait()
    copy.wait()
    out_ref[...] = node_update(mid, 1)


def body(*args):
    (grid, mesh, snd1, rcv1, feat1, tiles, lists, snd2, rcv2, feat2,
     sw, rw, ew, eb, mw, nw, nb, no, gain) = args
    gy, gx, width = grid.shape
    bands, lons = lax.axis_size("lat"), lax.axis_size("lon")
    patches = bands * lons
    nodes = mesh.shape[0]
    units = sw.shape[2]
    cap = lists.shape[0] // patches
    edges1, edges2 = snd1.shape[0], snd2.shape[0]
    cells = gy * gx
    ring = (gy + 2 * HALO) * (gx + 2 * HALO) - cells
    operands = [
        grid.reshape(cells, width), mesh, snd1.reshape(1, -1), rcv1.reshape(1, -1), feat1,
        tiles.reshape(1, -1), lists.reshape(1, -1), snd2.reshape(1, -1), rcv2.reshape(1, -1), feat2,
        sw, rw, ew, eb, mw, nw, nb, no, gain,
    ]
    shapes = [op.shape for op in operands]
    for i in (14, 15, 17):
        shapes[i] = (shapes[i][0], 2) + shapes[i][1:]
    shapes[16] = (2,) + shapes[16]
    held = [pltpu.VMEM(shape, op.dtype) for shape, op in zip(shapes, operands)]
    dma = pltpu.SemaphoreType.DMA
    scratch = held + [
        pltpu.VMEM((cells + nodes + FEAT_ROWS, units), BF),
        pltpu.VMEM((ring, units), BF),
        pltpu.VMEM((2 * gy * HALO, units), BF),
        pltpu.VMEM((cells + nodes + FEAT_ROWS, edges1), BF),
        pltpu.VMEM((ring, edges1), BF),
        pltpu.VMEM((units, edges1), F32),
        pltpu.VMEM((FEAT_ROWS, edges1), F32),
        pltpu.VMEM((2 * nodes + FEAT_ROWS, units), BF),
        pltpu.VMEM((patches, cap, units), F32),
        pltpu.VMEM((patches, cap, units), F32),
        pltpu.VMEM((2 * nodes + FEAT_ROWS, edges2), BF),
        pltpu.VMEM((patches * cap, edges2), BF),
        pltpu.VMEM((units, edges2), F32),
        pltpu.VMEM((FEAT_ROWS, edges2), F32),
        pltpu.VMEM((FEAT_ROWS, units), F32),
        pltpu.VMEM((2, 2, nodes, units), BF),
        dma((24,)), dma((7,)), dma((7,)), dma((8,)), dma((8,)), dma((2,)), dma((2,)),
        dma((patches,)), dma((patches,)),
    ]
    return pl.pallas_call(
        functools.partial(kernel, (bands, lons, gy, gx, cap)),
        out_shape=jax.ShapeDtypeStruct(mesh.shape, mesh.dtype),
        in_specs=[pl.BlockSpec(memory_space=pl.ANY)] * len(operands),
        out_specs=pl.BlockSpec(memory_space=pltpu.VMEM),
        scratch_shapes=scratch,
        compiler_params=pltpu.CompilerParams(
            collective_id=0, has_side_effects=True, vmem_limit_bytes=58 * 1024 * 1024
        ),
        name="encoder_processor",
    )(*operands)


def solution(mesh):
    placed = (
        P(("member", "lat"), "lon", None),
        P(("member", "lat", "lon"), None),
        P(("lat", "lon")),
        P(("lat", "lon")),
        P(None, ("lat", "lon")),
        P(("lat", "lon")),
        P(("lat", "lon")),
        P(("lat", "lon")),
        P(("lat", "lon")),
        P(None, ("lat", "lon")),
        P(None, None, "sub"),
        P(None, None, "sub"),
        P(None, None, "sub"),
        P(None, "sub"),
        P(None, "sub", None),
        P(None, None, "sub"),
        P(None, "sub"),
        P(None, "sub", None),
        P(),
    )
    return jax.shard_map(
        body,
        mesh=mesh,
        in_specs=placed,
        out_specs=P(("member", "lat", "lon"), None),
        check_vma=False,
    )
```

time: 172 us -> 27.5 us (0.16)
  waiting for transfers between devices: 95.7 us -> 0 us
  Pallas kernels: 0 us -> 25.7 us
  between operations: 16.3 us -> 0.01 us
  starting transfers between devices: 14.1 us -> 0 us
  matrix products: 13 us -> 0 us
  local copies, waits for them, and re-layouts: 14 us -> 1.67 us
  blocking collectives: 9.65 us -> 0 us
  other arithmetic: 7.26 us -> 0 us
    psum x2 -> x0, waiting for transfers between devices: 83.6 us -> none  [width_sum(): return lax.psum(partial_value, 'sub')]
    pallas_call x0 -> x1, Pallas kernels: none -> 25.7 us  [body(): pl.pallas_call(functools.partial(kernel, (bands, lons, gy, gx, cap)), out...]
    dot_general x15 -> x0, matrix products: 13 us -> none  [the longest x2 4.89 us: node_update(): jnp.dot(hidden, out_weight, preferred_element_type=jnp.float32)]
    gather x7 -> x0, local copies, waits for them, and re-layouts: 11.9 us -> none  [the longest x6 10.6 us: one_block(): preact = sender_table[send_ids].astype(jnp.float32) + recv_proj[recv_ids]]
    psum x2 -> x0, blocking collectives: 9.65 us -> none  [width_sum(): return lax.psum(partial_value, 'sub')]
    ppermute x4 -> x0, starting transfers between devices: 8.3 us -> none  [the longest x2 6.93 us: extended(): lax.ppermute(tail, axis, [(i, (i + 1) % count) for i in range(ends)])]
    all_to_all x1 -> x0, waiting for transfers between devices: 6.39 us -> none  [route(): lax.all_to_all(outgoing, ('lat', 'lon'), split_axis=0, concat_axis=0, til...]
    all_to_all x1 -> x0, starting transfers between devices: 5.78 us -> none  [route(): lax.all_to_all(outgoing, ('lat', 'lon'), split_axis=0, concat_axis=0, til...]
  transfers between devices with their start and end apart: 7 -> 0, of which waited for: 5 -> 0; matrix products, arithmetic and copies ran while one was open for 1% -> 0% of each run, Pallas kernels for 0% -> 0%
where the time goes in v1:
time: 27.5 us; the launch traced here: 27.4 us
  Pallas kernels  25.7 us (93%)
  local copies, waits for them, and re-layouts  1.67 us (6%)
    pallas_call x1, Pallas kernels, body(): pl.pallas_call(functools.partial(kernel, (bands, lons, gy, gx, cap)), out...  25.7 us
    unnamed x1, local copies, waits for them, and re-layouts  1.67 us

profile of v1, /device:TPU:0, one launch (start us, length us, event | category | flops | bytes accessed | tf_op | source)
XLA Modules:
  0.0 27.4 jit_solution(7119701248520123132)
XLA Ops:
  0.0 25.7 %encoder_processor.1 = bf16[256,512]{1,0:T(8,128)(2,1)} custom-call(bf16[512,512]{1,0:T(8,128)(2,1)} %bitcast.7, bf16[256,512]{1,0:T(8,128)(2,1)} %mesh_h.1, s32[1,1024]{1,0:T(1,128)} %bitcast.10, s32[1,1024]{1,0:T(1,128)} %bitcast.11, f32[4,1024]{1,0:T(4,128)} %feat1_h.1, s32[1,2]{1,0:T(1,128)} %bitcast.12, s32[1,64]{1,0:T(1,128)} %bitcast.13, ...), custom_call_target="tpu_custom_call" | custom-call | tf_op jit(solution)/shard_map/encoder_processor/pallas_call | solution.py:374
  25.7 1.7 %copy.21 = bf16[256,512]{1,0:T(8,128)(2,1)} copy(bf16[256,512]{1,0:T(8,128)(2,1)} %encoder_processor.1) | data formatting | bytes 524288

commit v2 on v1

--- a/solution.py
+++ b/solution.py
@@ -9,6 +9,7 @@
 
 HALO = 4
 TILE = 128
+SPAN = 512
 FEAT_ROWS = 16
 MESH = pl.DeviceIdType.MESH
 BF = jnp.bfloat16
@@ -57,8 +58,8 @@
     grid, mesh, snd1, rcv1, feat1, tiles, lists, snd2, rcv2, feat2,
     sw, rw, ew, eb, mw, nw, nb, no, gain,
     table1, halo, pack, hot1, hot1h, pre1, fs1,
-    table2, listed, arrived, hot2, hot2l, pre2, fs2, wf,
-    sums, local_sem, weight_send, weight_recv, halo_send, halo_recv, sum_send, sum_recv,
+    table2, listed, arrived, hot2, hot2f, hot2l, pre2, fs2, wf,
+    sums, fixed, relay, local_sem, weight_send, weight_recv, halo_send, halo_recv, sum_send, sum_recv,
     list_send, list_recv,
 ):
     bands, lons, gy, gx, cap = dims
@@ -80,16 +81,32 @@
         (mw_h.at[1], mw.at[1, sub]), (nw_h.at[1], nw.at[1, sub]), (no_h.at[1], no.at[1, sub]),
     ]
     local = [pltpu.make_async_copy(s, d, local_sem.at[i]) for i, (s, d) in enumerate(pairs)]
-    for copy in local:
+    for copy in local[:14]:
         copy.start()
+
+    turns = (0, 1) if lons == 2 else (0, 1, lons - 1)
+    has_n, has_s = lat > 0, lat < bands - 1
+    around = len(turns) - 1 + len(turns) * (has_n.astype(jnp.int32) + has_s.astype(jnp.int32))
+
+    def greet(sem):
+        for turn in turns[1:]:
+            pl.semaphore_signal(
+                sem, inc=1, device_id={"lon": lax.rem(lon + turn, lons)}, device_id_type=MESH
+            )
+        for there, shift in ((has_n, -1), (has_s, 1)):
+
+            @pl.when(there)
+            def _():
+                for turn in turns:
+                    pl.semaphore_signal(
+                        sem, inc=1, device_id={"lat": lat + shift, "lon": lax.rem(lon + turn, lons)},
+                        device_id_type=MESH,
+                    )
 
     barrier = pltpu.get_barrier_semaphore()
     pl.semaphore_signal(barrier, inc=1, device_id=peer, device_id_type=MESH)
-    for k in range(1, patches):
-        q = lax.rem(me + k, patches)
-        pl.semaphore_signal(
-            barrier, inc=1, device_id={"lat": q // lons, "lon": lax.rem(q, lons)}, device_id_type=MESH
-        )
+    greet(barrier)
+    rounds = max(bands - 2, lons // 2 - 1)
 
     for i in (0, 1):
         local[i].wait()
@@ -102,15 +119,15 @@
     choose = jnp.where(col == wanted, 1.0, 0.0).astype(BF)
     pack[...] = dot(choose, table1[0:cells, :]).astype(BF)
 
-    pl.semaphore_wait(barrier, patches)
+    for copy in local[14:]:
+        copy.start()
+    pl.semaphore_wait(barrier, around + 1)
 
     strip = HALO * gx
     half = HALO * HALO
     west = lax.rem(lon + lons - 1, lons)
     east = lax.rem(lon + 1, lons)
     base = 2 * strip
-    has_n, has_s = lat > 0, lat < bands - 1
-
     def halo_copy(i, src, dst, where):
         return pltpu.make_async_remote_copy(
             src_ref=src, dst_ref=halo.at[pl.ds(dst[0], dst[1])], send_sem=halo_send.at[i],
@@ -144,6 +161,7 @@
 
     for copy in across:
         copy.start()
+    greet(relay.at[0])
 
     weights = [
         pltpu.make_async_remote_copy(
@@ -225,9 +243,10 @@
     hot1[cells:cells + nodes, :] = one_hot(live(rcv1[...], 0), nodes)
     pre1[...] = dot_tn(table1[...], hot1[...])
 
-    hot2[2 * nodes:2 * nodes + FEAT_ROWS, :] = feature_rows(fs2, feat2)
+    hot2f[...] = feature_rows(fs2, feat2)
+    weights2 = weight_rows(1)
     rcv2[...] = live(rcv2[...], 1)
-    span = min(512, edges2)
+    span = min(SPAN, edges2)
 
     def select(step, carry):
         at = pl.ds(pl.multiple_of(step * span, span), span)
@@ -239,9 +258,26 @@
         turn = jnp.where(turn < 0, turn + patches, turn)
         ids = jnp.where(ids < nodes, -1, turn * cap + (ids - nodes) - source * cap)
         hot2l[:, at] = one_hot(ids, patches * cap)
+        pre2[:, at] = dot_tn(weights2, hot2f[:, at])
         return carry
 
     lax.fori_loop(0, edges2 // span, select, 0)
+
+    def latent_part(latent, layer):
+        for j in (0, 1):
+            fixed[layer, j] = dot(latent, nw[layer, j, 0:latent.shape[1], :]) + nb[j, layer:layer + 1, :]
+
+    def relayed(r):
+        pl.semaphore_wait(relay.at[r], around)
+        if r + 1 < rounds:
+            greet(relay.at[r + 1])
+
+    relayed(0)
+    for i in range(14, len(local)):
+        local[i].wait()
+    for other in weights[:4]:
+        other.wait()
+    latent_part(mesh[...], 0)
 
     @pl.when(has_n)
     def _():
@@ -272,19 +308,16 @@
 
     def node_update(latent, layer):
         inbound = dot(sums[layer, 0], mw[layer, 0]) + dot(sums[layer, 1], mw[layer, 1])
-        joined = jnp.concatenate([latent, inbound.astype(BF)], axis=1)
+        inbound = inbound.astype(BF)
         total = 0.0
         for j in (0, 1):
-            units = silu(dot(joined, nw[layer, j]) + nb[j, layer:layer + 1, :]).astype(BF)
+            units = silu(fixed[layer, j] + dot(inbound, nw[layer, j, latent.shape[1]:, :])).astype(BF)
             total = total + dot(units, no[layer, j])
         return (latent.astype(F32) + layer_norm(total) * gain[layer:layer + 1, :]).astype(BF)
 
     copy = exchange(0, dot_nt(hot1[cells:cells + nodes, :], hidden))
-    table2[2 * nodes:2 * nodes + FEAT_ROWS, :] = weight_rows(1)
-    for i in range(14, len(local)):
-        local[i].wait()
-    for other in weights[:4]:
-        other.wait()
+    for r in range(1, rounds):
+        relayed(r)
     copy.wait()
     mid = node_update(mesh[...], 0)
 
@@ -307,10 +340,13 @@
 
     def before(step, carry):
         at = pl.ds(pl.multiple_of(step * span, span), span)
-        pre2[:, at] = dot_tn(table2[...], hot2[:, at])
+        pre2[:, at] += dot_tn(table2[...], hot2[:, at])
         return carry
 
-    lax.fori_loop(0, edges2 // span, before, 0)
+    lax.fori_loop(0, edges2 // span, before, 0, unroll=True)
+    for other in weights[4:]:
+        other.wait()
+    latent_part(mid, 1)
     for route in routes:
         route.wait()
     far = arrived[...].reshape(patches * cap, arrived.shape[2]).astype(BF)
@@ -320,11 +356,8 @@
         hidden = silu(pre2[:, at] + dot_tn(far, hot2l[:, at])).astype(BF)
         return total + dot_nt(hot2[nodes:2 * nodes, at], hidden)
 
-    total = lax.fori_loop(0, edges2 // span, after, jnp.zeros((nodes, far.shape[1]), F32))
-    copy = exchange(1, total)
-    for other in weights[4:]:
-        other.wait()
-    copy.wait()
+    total = lax.fori_loop(0, edges2 // span, after, jnp.zeros((nodes, far.shape[1]), F32), unroll=True)
+    exchange(1, total).wait()
     out_ref[...] = node_update(mid, 1)
 
 
@@ -359,22 +392,25 @@
         pltpu.VMEM((ring, edges1), BF),
         pltpu.VMEM((units, edges1), F32),
         pltpu.VMEM((FEAT_ROWS, edges1), F32),
-        pltpu.VMEM((2 * nodes + FEAT_ROWS, units), BF),
+        pltpu.VMEM((2 * nodes, units), BF),
         pltpu.VMEM((patches, cap, units), F32),
         pltpu.VMEM((patches, cap, units), F32),
-        pltpu.VMEM((2 * nodes + FEAT_ROWS, edges2), BF),
+        pltpu.VMEM((2 * nodes, edges2), BF),
+        pltpu.VMEM((FEAT_ROWS, edges2), BF),
         pltpu.VMEM((patches * cap, edges2), BF),
         pltpu.VMEM((units, edges2), F32),
         pltpu.VMEM((FEAT_ROWS, edges2), F32),
         pltpu.VMEM((FEAT_ROWS, units), F32),
         pltpu.VMEM((2, 2, nodes, units), BF),
+        pltpu.VMEM((2, 2, nodes, units), F32),
+        pltpu.SemaphoreType.REGULAR((max(bands - 2, lons // 2 - 1),)),
         dma((24,)), dma((7,)), dma((7,)), dma((8,)), dma((8,)), dma((2,)), dma((2,)),
         dma((patches,)), dma((patches,)),
     ]
     return pl.pallas_call(
         functools.partial(kernel, (bands, lons, gy, gx, cap)),
         out_shape=jax.ShapeDtypeStruct(mesh.shape, mesh.dtype),
-        in_specs=[pl.BlockSpec(memory_space=pl.ANY)] * len(operands),
+        in_specs=[pl.BlockSpec(memory_space=pltpu.HBM)] * len(operands),
         out_specs=pl.BlockSpec(memory_space=pltpu.VMEM),
         scratch_shapes=scratch,
         compiler_params=pltpu.CompilerParams(

time: 27.5 us -> 24.5 us (0.89)
  Pallas kernels: 25.7 us -> 22.7 us
    pallas_call x1, Pallas kernels: 25.7 us -> 22.7 us  [body(): pl.pallas_call(functools.partial(kernel, (bands, lons, gy, gx, cap)), out...]
where the time goes in v2:
time: 24.5 us; the launch traced here: 24.4 us
  Pallas kernels  22.7 us (93%)
  local copies, waits for them, and re-layouts  1.67 us (7%)
    pallas_call x1, Pallas kernels, body(): pl.pallas_call(functools.partial(kernel, (bands, lons, gy, gx, cap)), out...  22.7 us
    unnamed x1, local copies, waits for them, and re-layouts  1.67 us

profile of v2, /device:TPU:0, one launch (start us, length us, event | category | flops | bytes accessed | tf_op | source)
XLA Modules:
  0.0 24.4 jit_solution(14901900448920543655)
XLA Ops:
  0.0 22.7 %encoder_processor.1 = bf16[256,512]{1,0:T(8,128)(2,1)} custom-call(bf16[512,512]{1,0:T(8,128)(2,1)} %bitcast.7, bf16[256,512]{1,0:T(8,128)(2,1)} %mesh_h.1, s32[1,1024]{1,0:T(1,128)} %bitcast.10, s32[1,1024]{1,0:T(1,128)} %bitcast.11, f32[4,1024]{1,0:T(4,128)} %feat1_h.1, s32[1,2]{1,0:T(1,128)} %bitcast.12, s32[1,64]{1,0:T(1,128)} %bitcast.13, ...), custom_call_target="tpu_custom_call" | custom-call | tf_op jit(solution)/shard_map/encoder_processor/pallas_call | solution.py:410
  22.7 1.7 %copy.21 = bf16[256,512]{1,0:T(8,128)(2,1)} copy(bf16[256,512]{1,0:T(8,128)(2,1)} %encoder_processor.1) | data formatting | bytes 524288
